TPU v7x, 256 devices: a whole 4x4x8 slice. The times are simulated.
256 devices in a mesh: gz: 16 (over z, core), row: 4 (over x), col: 4 (over y).
Axes of the slice: x: 4, y: 4, z: 8, core: 2. Of those that a mesh axis runs over, the one named last changes fastest.
Arguments:
- rhs_leaf: bfloat16 [2048, 256, 256], P(('gz', 'row', 'col')), may hold values from -6 to 6
- inv_leaf: bfloat16 [2048, 256, 256], P(('gz', 'row', 'col')), may hold values from -1 to 1.5, as said below
- couple_leaf: bfloat16 [2048, 1536, 256], P(('gz', 'row', 'col')), may hold values from -0.0625 to 0.0625
- pattern: int32 [2048, 12], P(('gz', 'row', 'col')), may hold values 0 or 1
- rhs_grid: bfloat16 [16, 1536, 256], P('gz', 'col'), may hold values from -6 to 6
- inv_grid: bfloat16 [16, 1536, 1536], P('gz', 'row', 'col'), may hold values from -1 to 1.5, as said below
- couple_grid: bfloat16 [16, 1024, 1536], P('gz', 'col', 'row'), may hold values from -0.0390625 to 0.0390625
- rhs_root: bfloat16 [1024, 256], P('col'), may hold values from -6 to 6
- inv_root: bfloat16 [1024, 1024], P('row', 'col'), may hold values from -1 to 1.5, as said below
Outputs:
- solve_leaf: float32 [2048, 256, 256], P(('gz', 'row', 'col'))
- solve_grid: float32 [16, 1536, 256], P('gz', 'col')
- solve_root: float32 [1024, 256], P('col')
Inputs may be any that keep to these rules, and one draw needn't show every extreme that they name: `inv_leaf`: each 256 x 256 block is lower triangular with a diagonal between 0.5 and 1.5. `inv_grid`: each 1536 x 1536 block is lower triangular with a diagonal between 0.5 and 1.5. `inv_root`: lower triangular with a diagonal between 0.5 and 1.5.
All inputs are finite; a program needn't handle non-finite values. No bound on the sum of `pattern` on one device may be relied on, other than what follows from the above.
Results may differ from a plain program's by a relative error of at most 0.0075.
Values may be sent and summed in bfloat16 or wider, within the bound.
A program may use at most 64 MiB of HBM per device.

v0:
```python
import jax
import jax.numpy as jnp
from jax import lax
from jax.sharding import PartitionSpec as P


def on_device(
    rhs_leaf, inv_leaf, couple_leaf, pattern, rhs_grid, inv_grid, couple_grid, rhs_root, inv_root
):
    block_rows = couple_leaf.shape[1] // pattern.shape[1]
    mask_rows = jnp.repeat(pattern, block_rows, axis=1).astype(jnp.bfloat16)
    masked = couple_leaf * mask_rows[:, :, None]
    leaf_half = jnp.einsum(
        "lij,ljk->lik", inv_leaf, rhs_leaf, preferred_element_type=jnp.float32
    ).astype(jnp.bfloat16)
    grid_cols = rhs_grid.shape[1]
    col_index = lax.axis_index("col")
    update_all = jnp.einsum("lgj,ljk->gk", masked, leaf_half, preferred_element_type=jnp.float32)
    summed = lax.psum(update_all, ("row", "col"))
    update = lax.dynamic_slice_in_dim(summed, col_index * grid_cols, grid_cols, 0)
    grid_res = (rhs_grid[0].astype(jnp.float32) - update).astype(jnp.bfloat16)
    grid_terms_fwd = jnp.dot(inv_grid[0], grid_res, preferred_element_type=jnp.float32)
    grid_half = lax.psum(grid_terms_fwd, "col").astype(jnp.bfloat16)
    root_terms = jnp.dot(couple_grid[0], grid_half, preferred_element_type=jnp.float32)
    root_update = lax.psum(root_terms, ("gz", "row"))
    root_res = (rhs_root.astype(jnp.float32) - root_update).astype(jnp.bfloat16)
    root_terms_fwd = jnp.dot(inv_root, root_res, preferred_element_type=jnp.float32)
    root_half = lax.psum(root_terms_fwd, "col").astype(jnp.bfloat16)
    root_terms_back = jnp.einsum(
        "ij,ik->jk", inv_root, root_half, preferred_element_type=jnp.float32
    )
    solve_root = lax.psum(root_terms_back, "row")
    back_half = solve_root.astype(jnp.bfloat16)
    coupled_terms = jnp.einsum(
        "ij,ik->jk", couple_grid[0], back_half, preferred_element_type=jnp.float32
    )
    coupled = lax.psum(coupled_terms, "col")
    grid_resid = (grid_half.astype(jnp.float32) - coupled).astype(jnp.bfloat16)
    grid_terms = jnp.einsum(
        "ij,ik->jk", inv_grid[0], grid_resid, preferred_element_type=jnp.float32
    )
    solve_grid = lax.psum(grid_terms, "row")
    whole_grid = lax.all_gather(solve_grid.astype(jnp.bfloat16), "col", axis=0, tiled=True)
    leaf_update = jnp.einsum("lgj,gk->ljk", masked, whole_grid, preferred_element_type=jnp.float32)
    leaf_back = (leaf_half.astype(jnp.float32) - leaf_update).astype(jnp.bfloat16)
    solve_leaf = jnp.einsum("lji,ljk->lik", inv_leaf, leaf_back, preferred_element_type=jnp.float32)
    return (solve_leaf, solve_grid[None], solve_root)


def solution(mesh):
    return jax.shard_map(
        on_device,
        mesh=mesh,
        in_specs=(
            P(("gz", "row", "col"), None, None),
            P(("gz", "row", "col"), None, None),
            P(("gz", "row", "col"), None, None),
            P(("gz", "row", "col"), None),
            P("gz", "col", None),
            P("gz", "row", "col"),
            P("gz", "col", "row"),
            P("col", None),
            P("row", "col"),
        ),
        out_specs=(P(("gz", "row", "col"), None, None), P("gz", "col", None), P("col", None)),
        check_vma=False,
    )
```

profile of v0, /device:TPU:1, one launch (start us, length us, event | category | flops | bytes accessed | tf_op | source)
XLA Modules:
  0.0 510.5 jit_solution(1147331615775888044)
XLA Ops:
  7.2 0.0 copy-start
  7.2 0.0 all-reduce.8.cloned.1.call-start
  7.2 0.8 convert_element_type.55
  8.0 0.1 copy.12
  8.1 0.1 broadcast_bitcast_fusion
  8.2 0.3 copy-done
  8.4 1.7 convolution_convert_fusion
  10.1 0.0 copy-start.2
  10.1 1.0 copy-done.2
  11.1 0.0 copy-start.1
  11.1 0.0 copy-start.5
  11.1 0.0 copy-start.3
  11.1 0.0 copy-start.4
  11.1 0.0 copy-start.6
  11.1 5.0 fusion.6
  16.0 0.0 all-reduce.8.cloned.1.call-update
  16.1 0.0 all-reduce.10.cloned.1.call-start
  16.1 101.3 %all-reduce.8.cloned.1.call-done = f32[1536,256]{1,0:T(8,128)} async-done(((f32[1536,256]{1,0:T(8,128)}), f32[1536,256]{1,0:T(8,128)}) %all-reduce.8.cloned.1.call-update) | async-done | bytes 1572880 | tf_op jit(solution)/shard_map/psum | solution.py:19
  117.4 0.0 copy-done.1
  117.4 0.0 copy-done.5
  117.4 1.3 convolution_bitcast_fusion.3
  118.7 16.5 %all-reduce.17 = bf16[384,256]{0,1:T(8,128)(2,1)S(1)} all-reduce(f32[384,256]{0,1:T(8,128)S(1)} %convolution_bitcast_fusion.3), channel_id=1, replica_groups=mesh['gz'=16,'row'=4,'col'=4] {'col'}, use_global_device_ids=true, to_apply=%region_1.0 | all-reduce | flops 98304 | bytes 589824 | tf_op jit(solution)/shard_map/psum | solution.py:23
  135.2 0.0 copy-done.3
  135.2 1.0 convolution_bitcast_fusion.4
  136.2 0.0 all-reduce.10.cloned.1.call-update
  136.2 0.0 all-reduce.12.cloned.1.call-start
  136.3 179.4 %all-reduce.10.cloned.1.call-done = f32[256,256]{1,0:T(8,128)} async-done(((f32[256,256]{1,0:T(8,128)}), f32[256,256]{1,0:T(8,128)}) %all-reduce.10.cloned.1.call-update) | async-done | bytes 262160 | tf_op jit(solution)/shard_map/psum | solution.py:25
  315.7 0.0 copy-done.4
  315.7 0.0 copy-done.6
  315.7 1.2 convolution_bitcast_fusion.6
  316.9 16.9 %all-reduce.18 = bf16[256,256]{0,1:T(8,128)(2,1)S(1)} all-reduce(f32[256,256]{0,1:T(8,128)S(1)} %convolution_bitcast_fusion.6), channel_id=1, replica_groups=mesh['gz'=16,'row'=4,'col'=4] {'col'}, use_global_device_ids=true, to_apply=%region_3.0 | all-reduce | flops 65536 | bytes 393216 | tf_op jit(solution)/shard_map/psum | solution.py:28
  333.8 0.9 convolution_bitcast_fusion.5
  334.7 0.0 all-reduce.12.cloned.1.call-update
  334.7 0.0 all-reduce.14.cloned.1.call-start
  334.7 43.3 %all-reduce.12.cloned.1.call-done = f32[256,256]{0,1:T(8,128)} async-done(((f32[256,256]{0,1:T(8,128)}), f32[256,256]{0,1:T(8,128)}) %all-reduce.12.cloned.1.call-update) | async-done | bytes 262160 | tf_op jit(solution)/shard_map/psum | solution.py:32
  378.0 1.9 convolution_bitcast_fusion.2
  380.0 0.0 all-reduce.14.cloned.1.call-update
  380.0 0.0 all-reduce.16.cloned.1.call-start
  380.0 48.8 %all-reduce.14.cloned.1.call-done = f32[384,256]{0,1:T(8,128)} async-done(((f32[384,256]{0,1:T(8,128)}), f32[384,256]{0,1:T(8,128)}) %all-reduce.14.cloned.1.call-update) | async-done | bytes 393232 | tf_op jit(solution)/shard_map/psum | solution.py:37
  428.9 2.0 convolution_bitcast_fusion.1
  430.9 0.0 all-reduce.16.cloned.1.call-update
  430.9 1.8 copy.16
  432.7 46.9 %all-reduce.16.cloned.1.call-done = f32[384,256]{0,1:T(8,128)} async-done(((f32[384,256]{0,1:T(8,128)}), f32[384,256]{0,1:T(8,128)}) %all-reduce.16.cloned.1.call-update) | async-done | bytes 393232 | tf_op jit(solution)/shard_map/psum | solution.py:42
  479.6 1.9 copy.15
  481.5 1.0 convert_element_type.67
  482.5 12.8 %all_gather.3 = bf16[1536,256]{0,1:T(8,128)(2,1)} all-gather(bf16[384,256]{0,1:T(8,128)(2,1)S(1)} %convert_element_type.67), channel_id=1, replica_groups=mesh['gz'=16,'row'=4,'col'=4] {'col'}, dimensions={0}, use_global_device_ids=true | all-gather | bytes 983040 | tf_op jit(solution)/shard_map/all_gather | solution.py:43
  495.3 6.8 %convolution_bitcast_fusion = f32[8,256,256]{1,2,0:T(8,128)S(1)} fusion(bf16[8,256,256]{2,1,0:T(8,128)(2,1)S(1)} %copy-done, bf16[8,256,256]{2,1,0:T(8,128)(2,1)} %copy-done.2, bf16[8,1536,256]{2,1,0:T(8,128)(2,1)} %param.11, bf16[8,1536]{1,0:T(8,128)(2,1)S(1)} %broadcast_bitcast_fusion, bf16[1536,256]{0,1:T(8,128)(2,1)} %all_gather.3), kind=kOutput, calls=%fused_computation.8 | convolution fusion | flops 1883766784 | bytes 11296768 | tf_op jit(solution)/shard_map/lji,ljk->lik/dot_general | solution.py:46
  502.1 1.8 copy.14
Async XLA Ops:
  7.2 1.2 copy-start
  7.2 110.2 %all-reduce.8.cloned.1.call-start = ((), (), s32[]{:S(2)}) async-start(), calls=%async_computation | async-start | bytes 3145728 | tf_op jit(solution)/shard_map/psum | solution.py:19
  10.1 1.0 copy-start.2
  11.1 106.3 %copy-start.1 = (bf16[1,384,384]{2,1,0:T(8,128)(2,1)S(1)}, bf16[1,384,384]{2,1,0:T(8,128)(2,1)}, u32[]{:S(2)}) copy-start(bf16[1,384,384]{2,1,0:T(8,128)(2,1)} %param.14) | copy-start | bytes 884740
  11.1 106.3 %copy-start.5 = (bf16[1,384,256]{2,1,0:T(8,128)(2,1)S(1)}, bf16[1,384,256]{2,1,0:T(8,128)(2,1)}, u32[]{:S(2)}) copy-start(bf16[1,384,256]{2,1,0:T(8,128)(2,1)} %param.13) | copy-start | bytes 589828
  11.1 124.2 %copy-start.3 = (bf16[1,256,384]{2,1,0:T(8,128)(2,1)S(1)}, bf16[1,256,384]{2,1,0:T(8,128)(2,1)}, u32[]{:S(2)}) copy-start(bf16[1,256,384]{2,1,0:T(8,128)(2,1)} %param.15) | copy-start | bytes 589828
  11.1 304.7 %copy-start.4 = (bf16[256,256]{1,0:T(8,128)(2,1)S(1)}, bf16[256,256]{1,0:T(8,128)(2,1)}, u32[]{:S(2)}) copy-start(bf16[256,256]{1,0:T(8,128)(2,1)} %param.17) | copy-start | bytes 393220
  11.1 304.7 %copy-start.6 = (bf16[256,256]{1,0:T(8,128)(2,1)S(1)}, bf16[256,256]{1,0:T(8,128)(2,1)}, u32[]{:S(2)}) copy-start(bf16[256,256]{1,0:T(8,128)(2,1)} %param.16) | copy-start | bytes 393220
  16.1 299.6 %all-reduce.10.cloned.1.call-start = ((), (), s32[]{:S(2)}) async-start(), calls=%async_computation.1 | async-start | bytes 524288 | tf_op jit(solution)/shard_map/psum | solution.py:25
  136.2 241.8 %all-reduce.12.cloned.1.call-start = ((), (), s32[]{:S(2)}) async-start(), calls=%async_computation.2 | async-start | bytes 524288 | tf_op jit(solution)/shard_map/psum | solution.py:32
  334.7 94.2 %all-reduce.14.cloned.1.call-start = ((), (), s32[]{:S(2)}) async-start(), calls=%async_computation.3 | async-start | bytes 786432 | tf_op jit(solution)/shard_map/psum | solution.py:37
  380.0 99.6 %all-reduce.16.cloned.1.call-start = ((), (), s32[]{:S(2)}) async-start(), calls=%async_computation.4 | async-start | bytes 786432 | tf_op jit(solution)/shard_map/psum | solution.py:42
Sparse Core Ops, SparseCore 0:
  16.2 101.1 all-reduce.7
  136.3 179.3 all-reduce.9
  334.8 43.1 all-reduce.11
  380.8 47.9 all-reduce.13
  431.7 47.8 all-reduce.15
where the time goes:
time: 515 us; the launch traced here: 510 us
  waiting for transfers between devices  420 us (82%)
  blocking collectives  46.2 us (9%)
  matrix products  21.6 us (4%)
  between operations  13.9 us (3%)
  local copies, waits for them, and re-layouts  6.92 us (1%)
    psum x1, waiting for transfers between devices, on_device(): root_update = lax.psum(root_terms, ('gz', 'row'))  179 us
    psum x1, waiting for transfers between devices, on_device(): summed = lax.psum(update_all, ('row', 'col'))  101 us
    psum x1, waiting for transfers between devices, on_device(): coupled = lax.psum(coupled_terms, 'col')  48.8 us
    psum x1, waiting for transfers between devices, on_device(): solve_grid = lax.psum(grid_terms, 'row')  46.9 us
    psum x1, waiting for transfers between devices, on_device(): solve_root = lax.psum(root_terms_back, 'row')  43.3 us
    psum x1, blocking collectives, on_device(): root_half = lax.psum(root_terms_fwd, 'col').astype(jnp.bfloat16)  16.9 us
    psum x1, blocking collectives, on_device(): grid_half = lax.psum(grid_terms_fwd, 'col').astype(jnp.bfloat16)  16.5 us
    all_gather x1, blocking collectives, on_device(): lax.all_gather(solve_grid.astype(jnp.bfloat16), 'col', axis=0, tiled=True)  12.8 us
  transfers between devices with their start and end apart: 5, of which 5 were waited for; matrix products, arithmetic and copies ran while one was open for 0% of the time, Pallas kernels for 0%

commit v1 on v0

v1 whole, which is shorter than its diff:
```python
import jax
import jax.numpy as jnp
from jax import lax
from jax.experimental import pallas as pl
from jax.experimental.pallas import tpu as pltpu
from jax.sharding import PartitionSpec as P

MESH = pl.DeviceIdType.MESH
F32 = jnp.float32
BF16 = jnp.bfloat16

NL = 8
N = 256
GB = 384
GP = 96
SG = 1536
RB = 256
NRHS = 256
SLICE = 16


def dot(a, b):
    return jnp.dot(a, b, preferred_element_type=F32)


def dot_nt(a, b):
    return lax.dot_general(a, b, (((1,), (1,)), ((), ())), preferred_element_type=F32)


def kernel(
    rhs_leaf, inv_leaf, couple_leaf, pattern, rhs_grid, inv_grid, couple_grid, rhs_root, inv_root,
    out_leaf, out_grid, out_root,
    rl, il, cl, fl, ct, ilt, ol,
    own1, snd1, rcv1, rg, part, psnd, rcv3, fg, coupleT, gridT,
    ut, usnd, rcv4, rootT_rhs, rcv5, wsnd, blocks, rr, rt, hsnd,
    csnd, rcv7, gb, qsnd, rcv8, xg,
    in_sems, leaf_sems, c_sems, out_sems, blk_sem,
    s1, r1, s2, r2, s3, r3, s3b, r3b, s4, r4, s5, r5, s6, r6, s7, r7, s7b, r7b, s8, r8, s9, r9,
    sR, rR, sC, rC,
):
    gz = lax.axis_index("gz")
    x = lax.axis_index("row")
    y = lax.axis_index("col")
    core = lax.rem(gz, 2)
    sibling = gz + 1 - 2 * core
    here = x * 4 + y

    def xpart(k):
        return (gz, lax.rem(x + k, 4), y)

    def ypart(k):
        return (gz, x, lax.rem(y + k, 4))

    def gpart(k):
        return (lax.rem(gz + k, 16), x, y)

    def ppart(k):
        return (gz, lax.rem(x + k // 4, 4), lax.rem(y + k % 4, 4))

    def remote(src, dst, ssem, rsem, dev):
        return pltpu.make_async_remote_copy(
            src_ref=src, dst_ref=dst, send_sem=ssem, recv_sem=rsem, device_id=dev, device_id_type=MESH
        )

    def rows(i, n):
        return pl.ds(pl.multiple_of(i * n, n), n)

    barrier = pltpu.get_barrier_semaphore()
    for k in range(1, 16):
        pl.semaphore_signal(barrier, inc=1, device_id=ppart(k), device_id_type=MESH)
        pl.semaphore_signal(barrier, inc=1, device_id=gpart(k), device_id_type=MESH)

    leaf_in = [
        pltpu.make_async_copy(rhs_leaf, rl, leaf_sems.at[0]),
        pltpu.make_async_copy(inv_leaf, il, leaf_sems.at[1]),
    ]
    for c in leaf_in:
        c.start()
    c_in = []
    for jj in range(4):
        block = rows(lax.rem(y + jj, 4), GB)
        c_in.append(pltpu.make_async_copy(couple_leaf.at[:, block], cl.at[:, block], c_sems.at[jj]))
        c_in[-1].start()
    half = pl.ds(pl.multiple_of(core * 128, 128), 128)
    own_block = pltpu.make_async_copy(inv_root.at[half], blocks.at[here, half], blk_sem)
    own_block.start()
    for c in leaf_in:
        c.wait()

    def leaf_fwd(l, carry):
        fl[rows(l, N), :] = dot(il[l], rl[l]).astype(BF16)
        return carry

    lax.fori_loop(0, NL, leaf_fwd, 0)
    pl.semaphore_wait(barrier, 30)

    sends = []
    for jj in range(4):
        b = lax.rem(y + jj, 4)
        c_in[jj].wait()
        parts = []
        for t in range(3):
            blk = pl.ds(pl.multiple_of(b * GB + t * 128, 128), 128)
            for l in range(NL):
                keep = pattern[l, b * 3 + t].astype(F32).astype(BF16)
                cl[l, blk, :] = cl[l, blk, :] * keep
        rb = rows(b, GB)
        acc = dot(jnp.concatenate([cl[l, rb, :] for l in range(NL)], axis=1), fl[...])
        if jj == 0:
            own1[...] = acc
        snd1[rows(jj, GB), :] = acc.astype(BF16)
        for dx in range(4):
            k = dx * 4 + jj
            if k == 0:
                continue
            piece = pl.ds(pl.multiple_of(jj * GB + lax.rem(x + dx, 4) * GP, 32), GP)
            c = remote(snd1.at[piece], rcv1.at[k], s1.at[k], r1.at[k], ppart(k))
            c.start()
            sends.append((k, c))

    own_block.wait()
    rsend = [
        remote(blocks.at[here, half], blocks.at[here, half], sR.at[k], rR.at[k], ppart(k))
        for k in range(1, 16)
    ]

    @pl.when(x >= y)
    def _():
        for c in rsend:
            c.start()

    def leaf_transpose(l, carry):
        ct[l] = cl[l].T
        ilt[l] = il[l].T
        return carry

    lax.fori_loop(0, NL, leaf_transpose, 0)
    coupleT[...] = couple_grid[0].T
    gridT[...] = inv_grid[0].T
    rootT_rhs[...] = rhs_root[...].astype(F32).T

    my_piece = rows(x, GP)
    tot = own1[my_piece, :]
    for k, c in sends:
        c.wait_recv()
    for k, c in sends:
        tot = tot + rcv1[k].astype(F32)
    rg[my_piece, :] = (rhs_grid[0, my_piece, :].astype(F32) - tot).astype(BF16)

    a2 = [remote(rg.at[my_piece], rg.at[my_piece], s2.at[k], r2.at[k], xpart(k)) for k in range(1, 4)]
    for c in a2:
        c.start()
    for c in a2:
        c.wait_recv()

    def reduce_y(partial, snd, rcv, ss, rs):
        part[...] = partial
        snd[...] = partial.astype(BF16)
        cs = [
            remote(snd.at[rows(lax.rem(y + k, 4), GP)], rcv.at[k], ss.at[k], rs.at[k], ypart(k))
            for k in range(1, 4)
        ]
        for c in cs:
            c.start()
        for c in cs:
            c.wait_recv()
        total = part[rows(y, GP), :]
        for k in range(1, 4):
            total = total + rcv[k].astype(F32)
        return total, cs

    def gather_y(buf, ss, rs):
        mine = rows(y, GP)
        cs = [remote(buf.at[mine], buf.at[mine], ss.at[k], rs.at[k], ypart(k)) for k in range(1, 4)]
        for c in cs:
            c.start()
        for c in cs:
            c.wait_recv()
        return cs

    total, a3 = reduce_y(dot(inv_grid[0], rg[...]), psnd, rcv3, s3, r3)
    fg[rows(y, GP), :] = total.astype(BF16)
    a3b = gather_y(fg, s3b, r3b)

    up = dot(couple_grid[0], fg[...]).T
    ut[...] = up
    usnd[...] = up.astype(BF16)
    a4 = [
        remote(usnd.at[rows(lax.rem(gz + k, 16), SLICE)], rcv4.at[k], s4.at[k], r4.at[k], gpart(k))
        for k in range(1, 16)
    ]
    for c in a4:
        c.start()

    for k in range(1, 16):
        @pl.when(lax.rem(x - k // 4 + 4, 4) >= lax.rem(y - k % 4 + 4, 4))
        def _():
            rsend[k - 1].wait_recv()
    pass_on = remote(blocks.at[:, half], blocks.at[:, half], sC.at[0], rC.at[0], (sibling, x, y))
    pass_on.start()

    for c in a4:
        c.wait_recv()
    mine = rows(gz, SLICE)
    v = ut[mine, :]
    for k in range(1, 16):
        v = v + rcv4[k].astype(F32)
    w = (jnp.where(x == 0, rootT_rhs[mine, :], 0.0) - v).astype(BF16)
    wsnd[...] = w
    rcv5[here] = w
    a5 = [remote(wsnd, rcv5.at[here], s5.at[k], r5.at[k], ppart(k)) for k in range(1, 16)]
    for c in a5:
        c.start()
    pass_on.wait_recv()
    for c in a5:
        c.wait_recv()
    res = []
    for j in range(4):
        t = rcv5[j].astype(F32)
        for i in range(1, 4):
            t = t + rcv5[i * 4 + j].astype(F32)
        res.append(t.astype(BF16))
    zs = []
    for i in range(4):
        t = dot_nt(res[0], blocks[i * 4])
        for j in range(1, i + 1):
            t = t + dot_nt(res[j], blocks[i * 4 + j])
        zs.append(t.astype(BF16))
    for j in range(4):
        t = dot(zs[j], blocks[j * 4 + j])
        for i in range(j + 1, 4):
            t = t + dot(zs[i], blocks[i * 4 + j])
        rr[j] = t.astype(BF16)
    hsnd[...] = rr[y]
    rt[mine, :] = rr[y]
    a6 = [remote(hsnd, rt.at[mine], s6.at[k], r6.at[k], gpart(k)) for k in range(1, 16)]
    for c in a6:
        c.start()
    for c in a6:
        c.wait_recv()
    root = rt[...].astype(F32).T
    out_root[...] = root

    total, a7 = reduce_y(dot(coupleT[...], root.astype(BF16)), csnd, rcv7, s7, r7)
    gb[rows(y, GP), :] = (fg[rows(y, GP), :].astype(F32) - total).astype(BF16)
    a7b = gather_y(gb, s7b, r7b)

    q = dot(gridT[...], gb[...])
    part[...] = q
    qsnd[...] = q.astype(BF16)
    a8 = [
        remote(qsnd.at[rows(lax.rem(x + k, 4), GP)], rcv8.at[k], s8.at[k], r8.at[k], xpart(k))
        for k in range(1, 4)
    ]
    for c in a8:
        c.start()
    for c in a8:
        c.wait_recv()
    total = part[my_piece, :]
    for k in range(1, 4):
        total = total + rcv8[k].astype(F32)
    home = rows(y * 4 + x, GP)
    xg[home, :] = total.astype(BF16)
    a9 = [remote(xg.at[home], xg.at[home], s9.at[k], r9.at[k], ppart(k)) for k in range(1, 16)]
    for c in a9:
        c.start()
    for c in a9:
        c.wait_recv()
    out_grid[0] = xg[rows(y, GB), :].astype(F32)

    for l in range(NL):
        back = (fl[l * N:(l + 1) * N, :].astype(F32) - dot(ct[l], xg[...])).astype(BF16)
        ol[l] = dot(ilt[l], back)
        pltpu.make_async_copy(ol.at[l], out_leaf.at[l], out_sems.at[l]).start()

    for k, c in sends:
        c.wait_send()

    @pl.when(x >= y)
    def _():
        for c in rsend:
            c.wait_send()

    for c in a2 + a3 + a3b + a4 + [pass_on] + a5 + a6 + a7 + a7b + a8 + a9:
        c.wait_send()
    for l in range(NL):
        pltpu.make_async_copy(ol.at[l], out_leaf.at[l], out_sems.at[l]).wait()


def on_device(*args):
    vm = pltpu.VMEM
    dma = pltpu.SemaphoreType.DMA
    vmem = pl.BlockSpec(memory_space=pltpu.VMEM)
    hbm = pl.BlockSpec(memory_space=pl.ANY)
    smem = pl.BlockSpec(memory_space=pltpu.SMEM)
    return pl.pallas_call(
        kernel,
        out_shape=(
            jax.ShapeDtypeStruct((NL, N, NRHS), F32),
            jax.ShapeDtypeStruct((1, GB, NRHS), F32),
            jax.ShapeDtypeStruct((RB, NRHS), F32),
        ),
        in_specs=[hbm, hbm, hbm, smem, vmem, vmem, vmem, vmem, hbm],
        out_specs=(hbm, vmem, vmem),
        scratch_shapes=[
            vm((NL, N, NRHS), BF16), vm((NL, N, N), BF16), vm((NL, SG, N), BF16),
            vm((NL * N, NRHS), BF16), vm((NL, N, SG), BF16), vm((NL, N, N), BF16),
            vm((NL, N, NRHS), F32),
            vm((GB, NRHS), F32), vm((SG, NRHS), BF16), vm((16, GP, NRHS), BF16),
            vm((GB, NRHS), BF16), vm((GB, NRHS), F32), vm((GB, NRHS), BF16),
            vm((4, GP, NRHS), BF16), vm((GB, NRHS), BF16), vm((GB, RB), BF16), vm((GB, GB), BF16),
            vm((NRHS, RB), F32), vm((NRHS, RB), BF16), vm((16, SLICE, RB), BF16),
            vm((NRHS, RB), F32), vm((16, SLICE, RB), BF16), vm((SLICE, RB), BF16),
            vm((16, RB, RB), BF16), vm((4, SLICE, RB), BF16), vm((NRHS, RB), BF16),
            vm((SLICE, RB), BF16),
            vm((GB, NRHS), BF16), vm((4, GP, NRHS), BF16), vm((GB, NRHS), BF16),
            vm((GB, NRHS), BF16), vm((4, GP, NRHS), BF16), vm((SG, NRHS), BF16),
            dma((8,)), dma((2,)), dma((4,)), dma((8,)), dma(()),
            dma((16,)), dma((16,)), dma((4,)), dma((4,)), dma((4,)), dma((4,)), dma((4,)), dma((4,)),
            dma((16,)), dma((16,)), dma((16,)), dma((16,)), dma((16,)), dma((16,)),
            dma((4,)), dma((4,)), dma((4,)), dma((4,)), dma((4,)), dma((4,)), dma((16,)), dma((16,)),
            dma((16,)), dma((16,)), dma((1,)), dma((1,)),
        ],
        compiler_params=pltpu.CompilerParams(
            collective_id=0, has_side_effects=True, vmem_limit_bytes=48 << 20
        ),
        cost_estimate=pl.CostEstimate(flops=4_200_000_000, bytes_accessed=13_000_000, transcendentals=0),
        name="solve",
    )(*args)


def solution(mesh):
    return jax.shard_map(
        on_device,
        mesh=mesh,
        in_specs=(
            P(("gz", "row", "col"), None, None),
            P(("gz", "row", "col"), None, None),
            P(("gz", "row", "col"), None, None),
            P(("gz", "row", "col"), None),
            P("gz", "col", None),
            P("gz", "row", "col"),
            P("gz", "col", "row"),
            P("col", None),
            P("row", "col"),
        ),
        out_specs=(P(("gz", "row", "col"), None, None), P("gz", "col", None), P("col", None)),
        check_vma=False,
    )
```

time: 515 us -> 107 us (0.21)
  waiting for transfers between devices: 420 us -> 0 us
  Pallas kernels: 0 us -> 93.4 us
  blocking collectives: 46.2 us -> 0 us
  matrix products: 21.6 us -> 0 us
  between operations: 13.9 us -> 0.66 us
    psum x5 -> x0, waiting for transfers between devices: 420 us -> none  [the longest x1 179 us: on_device(): root_update = lax.psum(root_terms, ('gz', 'row'))]
    pallas_call x0 -> x1, Pallas kernels: none -> 93.4 us  [on_device(): pl.pallas_call(kernel, out_shape=(jax.ShapeDtypeStruct((NL, N, NRHS), F32...]
    psum x2 -> x0, blocking collectives: 33.4 us -> none  [the longest x1 16.9 us: on_device(): root_half = lax.psum(root_terms_fwd, 'col').astype(jnp.bfloat16)]
    dot_general x9 -> x0, matrix products: 21.6 us -> none  [the longest x1 6.76 us: on_device(): jnp.einsum('lji,ljk->lik', inv_leaf, leaf_back, preferred_element_type=jn...]
    all_gather x1 -> x0, blocking collectives: 12.8 us -> none  [on_device(): lax.all_gather(solve_grid.astype(jnp.bfloat16), 'col', axis=0, tiled=True)]
    unnamed x17 -> x19, local copies, waits for them, and re-layouts: 6.75 us -> 10.5 us
  transfers between devices with their start and end apart: 5 -> 0, of which waited for: 5 -> 0; matrix products, arithmetic and copies ran while one was open for 0% -> 0% of each run, Pallas kernels for 0% -> 0%
where the time goes in v1:
time: 107 us; the launch traced here: 105 us
  Pallas kernels  93.4 us (87%)
  local copies, waits for them, and re-layouts  10.5 us (10%)
    pallas_call x1, Pallas kernels, on_device(): pl.pallas_call(kernel, out_shape=(jax.ShapeDtypeStruct((NL, N, NRHS), F32...  93.4 us
    unnamed x19, local copies, waits for them, and re-layouts  10.5 us

profile of v1, /device:TPU:1, one launch (start us, length us, event | category | flops | bytes accessed | tf_op | source)
XLA Modules:
  0.0 104.5 jit_solution(18107900764990694063)
XLA Ops:
  0.6 0.0 copy-start
  0.6 1.2 %copy-done = bf16[8,256,256]{2,1,0:T(8,128)(2,1)S(1)} copy-done((bf16[8,256,256]{2,1,0:T(8,128)(2,1)S(1)}, bf16[8,256,256]{2,1,0:T(8,128)(2,1)}, u32[]{:S(2)}) %copy-start) | copy-done | bytes 1048600
  1.9 0.0 copy-start.1
  1.9 1.2 %copy-done.1 = bf16[8,256,256]{2,1,0:T(8,128)(2,1)S(1)} copy-done((bf16[8,256,256]{2,1,0:T(8,128)(2,1)S(1)}, bf16[8,256,256]{2,1,0:T(8,128)(2,1)}, u32[]{:S(2)}) %copy-start.1) | copy-done | bytes 1048600
  3.1 0.0 copy-start.2
  3.1 1.0 copy-done.2
  4.0 0.0 copy-start.3
  4.0 0.9 copy-done.3
  5.0 0.0 copy-start.4
  5.0 0.9 copy-done.4
  5.9 0.0 copy-start.5
  5.9 0.9 copy-done.5
  6.8 0.0 copy-start.6
  6.8 0.9 copy-done.6
  7.7 0.0 copy-start.7
  7.7 0.7 copy-done.7
  8.4 93.4 %solve.1 = (f32[8,256,256]{2,1,0:T(8,128)S(1)}, f32[1,384,256]{2,1,0:T(8,128)S(1)}, f32[256,256]{1,0:T(8,128)S(1)}) custom-call(bf16[8,256,256]{2,1,0:T(8,128)(2,1)S(1)} %copy-done, bf16[8,256,256]{2,1,0:T(8,128)(2,1)S(1)} %copy-done.1, bf16[8,1536,256]{2,1,0:T(8,128)(2,1)} %couple_leaf.1, s32[8,12]{1,0:T(8,128)S(1)} %copy-done.7, ...), custom_call_target="tpu_custom_call" | custom-call | flops 4200000000 | bytes 13000000 | tf_op jit(solution)/shard_map/solve/pallas_call | solution.py:296
  101.8 1.3 %copy.15 = f32[8,256,256]{2,1,0:T(8,128)} copy(f32[8,256,256]{2,1,0:T(8,128)S(1)} %get-tuple-element.6) | data formatting | bytes 4194304
  103.1 0.7 copy.16
  103.8 0.7 copy.17
Async XLA Ops:
  0.6 1.2 %copy-start = (bf16[8,256,256]{2,1,0:T(8,128)(2,1)S(1)}, bf16[8,256,256]{2,1,0:T(8,128)(2,1)}, u32[]{:S(2)}) copy-start(bf16[8,256,256]{2,1,0:T(8,128)(2,1)} %rhs_leaf.1) | copy-start | bytes 3145732
  1.9 1.2 %copy-start.1 = (bf16[8,256,256]{2,1,0:T(8,128)(2,1)S(1)}, bf16[8,256,256]{2,1,0:T(8,128)(2,1)}, u32[]{:S(2)}) copy-start(bf16[8,256,256]{2,1,0:T(8,128)(2,1)} %inv_leaf.1) | copy-start | bytes 3145732
  3.1 1.0 copy-start.2
  4.0 0.9 copy-start.3
  5.0 0.9 copy-start.4
  5.9 0.9 copy-start.5
  6.8 0.9 copy-start.6
  7.7 0.7 copy-start.7

commit v2 on v0

v2 whole, which is shorter than its diff:
```python
import jax
import jax.numpy as jnp
from jax import lax
from jax.experimental import pallas as pl
from jax.experimental.pallas import tpu as pltpu
from jax.sharding import PartitionSpec as P

MESH = pl.DeviceIdType.MESH
F32 = jnp.float32
BF16 = jnp.bfloat16

NL = 8
N = 256
GB = 384
GP = 96
SG = 1536
RB = 256
NRHS = 256
HALF = SG // 2
SLICE = 16


def dot(a, b):
    return jnp.dot(a, b, preferred_element_type=F32)


def dot_nt(a, b):
    return lax.dot_general(a, b, (((1,), (1,)), ((), ())), preferred_element_type=F32)


def dot_tn(a, b):
    return lax.dot_general(a, b, (((0,), (0,)), ((), ())), preferred_element_type=F32)


def kernel(
    rhs_leaf, inv_leaf, couple_leaf, pattern, rhs_grid, inv_grid, couple_grid, rhs_root, inv_root,
    out_back, out_top, out_root,
    rl, il, cl, fl, ct, ol, back, xg, lg, rgrid, rroot,
    cg, bsnd, rcvb, bacc, bm, btm, bts,
    own1, snd1, rcv1, rg, part, psnd, rcv3, fg, gridT, hpart, hsnd, rcv8,
    ut, usnd, rcv4, rootT_rhs, rcv5, wsnd, blocks, rt,
    in_sems, c_sems, out_sems,
    s1, r1, s2, r2, s3, r3, s3b, r3b, s4, r4, s5, r5, s6, r6, s8, r8, s9, r9,
    sR, rR, sC, rC, sG, rG, sB, rB, sT, rT,
):
    gz = lax.axis_index("gz")
    x = lax.axis_index("row")
    y = lax.axis_index("col")
    core = lax.rem(gz, 2)
    sibling = (gz + 1 - 2 * core, x, y)
    here = x * 4 + y

    def xpart(k):
        return (gz, lax.rem(x + k, 4), y)

    def ypart(k):
        return (gz, x, lax.rem(y + k, 4))

    def gpart(k):
        return (lax.rem(gz + k, 16), x, y)

    def ppart(k):
        return (gz, lax.rem(x + k // 4, 4), lax.rem(y + k % 4, 4))

    def remote(src, dst, ssem, rsem, dev):
        return pltpu.make_async_remote_copy(
            src_ref=src, dst_ref=dst, send_sem=ssem, recv_sem=rsem, device_id=dev, device_id_type=MESH
        )

    def rows(i, n):
        return pl.ds(pl.multiple_of(i * n, n), n)

    pending = []

    def start(copies, when=None):
        for c in copies:
            if when is None:
                c.start()
            else:
                pl.when(when)(c.start)
            pending.append((c, when))

    def arrived(copies, when=None):
        for c in copies:
            if when is None:
                c.wait_recv()
            else:
                pl.when(when)(c.wait_recv)

    def finish():
        for c, when in pending:
            if when is None:
                c.wait_send()
            else:
                pl.when(when)(c.wait_send)

    mine = rows(gz, SLICE)
    mine_root = x * (x + 1) // 2 + y
    load_r = pltpu.make_async_copy(rhs_leaf, rl, in_sems.at[0])
    load_i = pltpu.make_async_copy(inv_leaf, il, in_sems.at[1])
    load_r.start()
    load_i.start()
    load_c = []
    for jj in range(4):
        block = rows(lax.rem(y + jj, 4), GB)
        load_c.append(pltpu.make_async_copy(couple_leaf.at[:, block], cl.at[:, block], c_sems.at[jj]))
        load_c[-1].start()
    loads = [
        pltpu.make_async_copy(couple_grid.at[0], cg.at[y], in_sems.at[2]),
        pltpu.make_async_copy(inv_grid.at[0], lg, in_sems.at[3]),
        pltpu.make_async_copy(rhs_grid.at[0], rgrid, in_sems.at[4]),
        pltpu.make_async_copy(rhs_root, rroot, in_sems.at[5]),
    ]
    for c in loads:
        c.start()
    load_b = pltpu.make_async_copy(inv_root.at[mine], blocks.at[mine_root, mine], in_sems.at[6])
    pl.when(x >= y)(load_b.start)

    barrier = pltpu.get_barrier_semaphore()
    for k in range(1, 16):
        pl.semaphore_signal(barrier, inc=1, device_id=ppart(k), device_id_type=MESH)
        pl.semaphore_signal(barrier, inc=1, device_id=gpart(k), device_id_type=MESH)

    load_r.wait()
    load_i.wait()

    for l in range(NL):
        fl[l * N:(l + 1) * N, :] = dot(il[l], rl[l]).astype(BF16)

    a1 = []
    for jj in range(4):
        b = lax.rem(y + jj, 4)
        load_c[jj].wait()
        for t in range(3):
            blk = pl.ds(pl.multiple_of(b * GB + t * 128, 128), 128)
            for l in range(NL):
                keep = pattern[l, b * 3 + t].astype(F32).astype(BF16)
                cl[l, blk, :] = cl[l, blk, :] * keep
        rb = rows(b, GB)
        acc = dot(jnp.concatenate([cl[l, rb, :] for l in range(NL)], axis=1), fl[...])
        if jj == 0:
            own1[...] = acc
        snd1[rows(jj, GB), :] = acc.astype(BF16)
        if jj == 1:
            pl.semaphore_wait(barrier, 30)
        for sent in {0: (), 1: (0, 1), 2: (2,), 3: (3,)}[jj]:
            for dx in range(4):
                k = dx * 4 + sent
                if k == 0:
                    continue
                piece = pl.ds(pl.multiple_of(sent * GB + lax.rem(x + dx, 4) * GP, 32), GP)
                a1.append(remote(snd1.at[piece], rcv1.at[k], s1.at[k], r1.at[k], ppart(k)))
                start(a1[-1:])

    pl.when(x >= y)(load_b.wait)
    rsend = [
        remote(blocks.at[mine_root, mine], blocks.at[mine_root, mine], sR.at[k], rR.at[k], ppart(k))
        for k in range(1, 16)
    ]
    start(rsend, x >= y)

    def leaf_transpose(l, carry):
        ct[l] = cl[l].T
        return carry

    lax.fori_loop(0, 2, leaf_transpose, 0)
    for c in loads:
        c.wait()
    gridT[...] = lg[...].T
    rootT_rhs[...] = rroot[...].astype(F32).T
    for k in range(1, 16):
        arrived([rsend[k - 1]], lax.rem(x - k // 4 + 4, 4) >= lax.rem(y - k % 4 + 4, 4))
    zsend = [
        remote(blocks.at[:, mine], blocks.at[:, mine], sC.at[k], rC.at[k], gpart(k)) for k in range(2, 16, 2)
    ]
    zpass = [remote(blocks.at[:, mine], blocks.at[:, mine], sC.at[1], rC.at[1], sibling)]
    start(zsend)
    start(zpass)
    my_piece = rows(x, GP)
    arrived(a1)
    tot = own1[my_piece, :]
    for k in range(1, 16):
        tot = tot + rcv1[k].astype(F32)
    rg[my_piece, :] = (rgrid[my_piece, :].astype(F32) - tot).astype(BF16)

    a2 = [remote(rg.at[my_piece], rg.at[my_piece], s2.at[k], r2.at[k], xpart(k)) for k in range(1, 4)]
    start(a2)
    lax.fori_loop(2, 4, leaf_transpose, 0)
    arrived(a2)
    partial = dot(lg[...], rg[...])
    part[...] = partial
    psnd[...] = partial.astype(BF16)
    a3 = [
        remote(psnd.at[rows(lax.rem(y + k, 4), GP)], rcv3.at[k], s3.at[k], r3.at[k], ypart(k))
        for k in range(1, 4)
    ]
    start(a3)
    lax.fori_loop(4, 6, leaf_transpose, 0)
    my_rows = rows(y, GP)
    arrived(a3)
    total = part[my_rows, :]
    for k in range(1, 4):
        total = total + rcv3[k].astype(F32)
    fg[my_rows, :] = total.astype(BF16)
    a3b = [remote(fg.at[my_rows], fg.at[my_rows], s3b.at[k], r3b.at[k], ypart(k)) for k in range(1, 4)]
    start(a3b)
    gsend = [remote(couple_grid.at[0], cg.at[y], sG.at[k], rG.at[k], ypart(k)) for k in range(1, 4)]

    for k in range(1, 4):
        start([gsend[k - 1]], lax.rem(y + k, 4) <= x)
    lax.fori_loop(6, 8, leaf_transpose, 0)
    arrived(a3b)
    up = dot(cg[y], fg[...]).T
    ut[...] = up
    usnd[...] = up.astype(BF16)
    a4 = [
        remote(usnd.at[rows(lax.rem(gz + k, 16), SLICE)], rcv4.at[k], s4.at[k], r4.at[k], gpart(k))
        for k in range(1, 16)
    ]
    start(a4)
    partial = dot(gridT[...], fg[...])
    hpart[...] = partial
    hsnd[...] = partial.astype(BF16)
    a8 = [
        remote(hsnd.at[rows(lax.rem(x + k, 4), GP)], rcv8.at[k], s8.at[k], r8.at[k], xpart(k))
        for k in range(1, 4)
    ]
    start(a8)
    for i, k in enumerate(range(2, 16, 2)):
        arrived([zsend[i]])
        from_z = rows(lax.rem(gz - k + 16, 16), SLICE)
        zpass.append(remote(blocks.at[:, from_z], blocks.at[:, from_z], sC.at[k + 1], rC.at[k + 1], sibling))
        start(zpass[-1:])
    arrived(gsend, y <= x)

    @pl.when(y <= x)
    def _():
        for a in range(4):
            bsnd[a] = dot(cg[a], lg[...]).astype(BF16)

    bsend = [
        remote(bsnd.at[lax.rem(x + k, 4)], rcvb.at[k], sB.at[k], rB.at[k], xpart(k)) for k in range(1, 4)
    ]
    start(bsend, y <= x)
    arrived(a4)
    v = ut[mine, :]
    for k in range(1, 16):
        v = v + rcv4[k].astype(F32)
    w = (jnp.where(x == 0, rootT_rhs[mine, :], 0.0) - v).astype(BF16)
    wsnd[...] = w
    rcv5[here] = w
    a5 = [remote(wsnd, rcv5.at[here], s5.at[k], r5.at[k], ppart(k)) for k in range(1, 16)]
    start(a5)
    arrived(a8)
    hpart[my_piece, :] += rcv8[1].astype(F32) + rcv8[2].astype(F32) + rcv8[3].astype(F32)
    arrived(zpass)
    arrived(a5)
    res = []
    for j in range(4):
        t = rcv5[j].astype(F32)
        for i in range(1, 4):
            t = t + rcv5[i * 4 + j].astype(F32)
        res.append(t.astype(BF16))
    zs = []
    for i in range(4):
        t = dot_nt(res[0], blocks[i * (i + 1) // 2])
        for j in range(1, i + 1):
            t = t + dot_nt(res[j], blocks[i * (i + 1) // 2 + j])
        zs.append(t.astype(BF16))
    for j in range(4):
        t = dot(zs[j], blocks[j * (j + 1) // 2 + j])
        for i in range(j + 1, 4):
            t = t + dot(zs[i], blocks[i * (i + 1) // 2 + j])
        rt[mine, j * RB:(j + 1) * RB] = t.astype(BF16)

    a6 = [remote(rt.at[mine], rt.at[mine], s6.at[k], r6.at[k], gpart(k)) for k in range(2, 16, 2)]
    start(a6)
    a6b = [remote(rt.at[mine], rt.at[mine], s6.at[1], r6.at[1], sibling)]
    start(a6b)
    bacc[...] = jnp.zeros_like(bacc)

    @pl.when(y <= x)
    def _():
        bacc[...] = bsnd[x].astype(F32)

    for k in range(1, 4):
        sent = lax.rem(x - k + 4, 4) >= y
        arrived([bsend[k - 1]], sent)

        @pl.when(sent)
        def _():
            bacc[...] += rcvb[k].astype(F32)

    bm[...] = bacc[...].astype(BF16)
    btm[...] = bm[...].T
    bts[x] = btm[my_piece, :]
    at = [
        remote(btm.at[rows(lax.rem(x + k, 4), GP)], bts.at[x], sT.at[k], rT.at[k], xpart(k))
        for k in range(1, 4)
    ]
    start(at)
    for i, k in enumerate(range(2, 16, 2)):
        arrived([a6[i]])
        from_z = rows(lax.rem(gz - k + 16, 16), SLICE)
        a6b.append(
            remote(rt.at[from_z], rt.at[from_z], s6.at[k + 1], r6.at[k + 1], sibling)
        )
        start(a6b[-1:])
    arrived(at)
    arrived(a6b)
    h = hpart[my_piece, :]
    for i in range(4):
        h = h - dot_nt(bts[i], rt[:, i * RB:(i + 1) * RB])
    home = rows(y * 4 + x, GP)
    xg[home, :] = h.astype(BF16)
    a9 = [remote(xg.at[home], xg.at[home], s9.at[k], r9.at[k], ppart(k)) for k in range(1, 16)]
    start(a9)
    stores = [pltpu.make_async_copy(rt.at[:, rows(y, RB)], out_root, out_sems.at[2])]
    stores[0].start()
    odd = lax.rem(y, 2) == 1
    for k in range(1, 16):
        dy = k % 4
        if dy == 0:
            arrived(a9[k - 1:k])
        elif dy == 1:
            arrived(a9[k - 1:k], odd)
        elif dy == 3:
            arrived(a9[k - 1:k], jnp.logical_not(odd))
    top = pl.ds(pl.multiple_of((y // 2) * HALF, HALF), HALF)
    for g in range(2):
        ls = slice(g * 4, g * 4 + 4)
        t = dot(ct[ls, :, top].reshape(4 * N, HALF), xg[top, :])
        gs = slice(g * 4 * N, (g + 1) * 4 * N)
        ol[gs, :] = fl[gs, :].astype(F32) - t
    for k in range(1, 16):
        dy = k % 4
        if dy == 2:
            arrived(a9[k - 1:k])
        elif dy == 1:
            arrived(a9[k - 1:k], jnp.logical_not(odd))
        elif dy == 3:
            arrived(a9[k - 1:k], odd)
    rest = pl.ds(pl.multiple_of((1 - y // 2) * HALF, HALF), HALF)
    for g in range(2):
        gs = slice(g * 4 * N, (g + 1) * 4 * N)
        t = dot(ct[g * 4:g * 4 + 4, :, rest].reshape(4 * N, HALF), xg[rest, :])
        back[gs, :] = (ol[gs, :] - t).astype(BF16)
        stores.append(pltpu.make_async_copy(back.at[gs], out_back.at[gs], out_sems.at[g]))
        stores[-1].start()
    stores.append(pltpu.make_async_copy(xg.at[rows(y, GB)], out_top, out_sems.at[3]))
    stores[-1].start()
    finish()
    for c in stores:
        c.wait()


def leaves_back(
    inv_leaf, res_leaf, top, root, out_leaf, out_grid, out_root,
    il, bk, tp, rt, sol, og, oroot, i_sems, b_sems, sems,
):
    loads = []
    for l in range(NL):
        loads.append((
            pltpu.make_async_copy(inv_leaf.at[l], il.at[l], i_sems.at[l]),
            pltpu.make_async_copy(res_leaf.at[pl.ds(l * N, N)], bk.at[l], b_sems.at[l]),
        ))
        for c in loads[l]:
            c.start()
    small = [pltpu.make_async_copy(top, tp, sems.at[NL + 2]), pltpu.make_async_copy(root, rt, sems.at[NL + 3])]
    for c in small:
        c.start()
    copies = []
    for l in range(NL):
        for c in loads[l]:
            c.wait()
        sol[l] = dot_tn(il[l], bk[l])
        copies.append(pltpu.make_async_copy(sol.at[l], out_leaf.at[l], sems.at[l]))
        copies[-1].start()
    for c in small:
        c.wait()
    og[...] = tp[...].astype(F32)
    copies.append(pltpu.make_async_copy(og, out_grid.at[0], sems.at[NL]))
    copies[-1].start()
    oroot[...] = rt[...].astype(F32).T
    copies.append(pltpu.make_async_copy(oroot, out_root, sems.at[NL + 1]))
    copies[-1].start()
    for c in copies:
        c.wait()


def on_device(*args):
    vm = pltpu.VMEM
    dma = pltpu.SemaphoreType.DMA
    hbm = pl.BlockSpec(memory_space=pl.ANY)
    smem = pl.BlockSpec(memory_space=pltpu.SMEM)
    kept = pl.pallas_call(
        kernel,
        out_shape=(
            jax.ShapeDtypeStruct((NL * N, NRHS), BF16),
            jax.ShapeDtypeStruct((GB, NRHS), BF16),
            jax.ShapeDtypeStruct((NRHS, RB), BF16),
        ),
        in_specs=[hbm, hbm, hbm, smem, hbm, hbm, hbm, hbm, hbm],
        out_specs=(hbm, hbm, hbm),
        scratch_shapes=[
            vm((NL, N, NRHS), BF16), vm((NL, N, N), BF16), vm((NL, SG, N), BF16),
            vm((NL * N, NRHS), BF16), vm((NL, N, SG), BF16), vm((NL * N, NRHS), F32),
            vm((NL * N, NRHS), BF16), vm((SG, NRHS), BF16), vm((GB, GB), BF16), vm((GB, NRHS), BF16), vm((RB, NRHS), BF16),
            vm((4, RB, GB), BF16), vm((4, RB, GB), BF16), vm((4, RB, GB), BF16), vm((RB, GB), F32),
            vm((RB, GB), BF16), vm((GB, RB), BF16), vm((4, GP, RB), BF16),
            vm((GB, NRHS), F32), vm((SG, NRHS), BF16), vm((16, GP, NRHS), BF16),
            vm((GB, NRHS), BF16), vm((GB, NRHS), F32), vm((GB, NRHS), BF16),
            vm((4, GP, NRHS), BF16), vm((GB, NRHS), BF16), vm((GB, GB), BF16),
            vm((GB, NRHS), F32), vm((GB, NRHS), BF16), vm((4, GP, NRHS), BF16),
            vm((NRHS, RB), F32), vm((NRHS, RB), BF16), vm((16, SLICE, RB), BF16),
            vm((NRHS, RB), F32), vm((16, SLICE, RB), BF16), vm((SLICE, RB), BF16),
            vm((10, RB, RB), BF16), vm((NRHS, 4 * RB), BF16),
            dma((7,)), dma((4,)), dma((4,)),
            dma((16,)), dma((16,)), dma((4,)), dma((4,)), dma((4,)), dma((4,)), dma((4,)), dma((4,)),
            dma((16,)), dma((16,)), dma((16,)), dma((16,)), dma((16,)), dma((16,)),
            dma((4,)), dma((4,)), dma((16,)), dma((16,)),
            dma((16,)), dma((16,)), dma((16,)), dma((16,)), dma((4,)), dma((4,)), dma((4,)), dma((4,)),
            dma((4,)), dma((4,)),
        ],
        compiler_params=pltpu.CompilerParams(
            collective_id=0, has_side_effects=True, vmem_limit_bytes=62 << 20
        ),
        cost_estimate=pl.CostEstimate(flops=4_200_000_000, bytes_accessed=13_000_000, transcendentals=0),
        name="solve",
    )(*args)
    return pl.pallas_call(
        leaves_back,
        out_shape=(
            jax.ShapeDtypeStruct((NL, N, NRHS), F32),
            jax.ShapeDtypeStruct((1, GB, NRHS), F32),
            jax.ShapeDtypeStruct((RB, NRHS), F32),
        ),
        in_specs=[hbm] * 4,
        out_specs=(hbm, hbm, hbm),
        scratch_shapes=[
            vm((NL, N, N), BF16), vm((NL, N, NRHS), BF16), vm((GB, NRHS), BF16), vm((NRHS, RB), BF16),
            vm((NL, N, NRHS), F32), vm((GB, NRHS), F32), vm((RB, NRHS), F32),
            dma((NL,)), dma((NL,)), dma((NL + 4,)),
        ],
        compiler_params=pltpu.CompilerParams(vmem_limit_bytes=62 << 20),
        cost_estimate=pl.CostEstimate(flops=270_000_000, bytes_accessed=4_800_000, transcendentals=0),
        name="leaves_back",
    )(args[1], *kept)


def solution(mesh):
    return jax.shard_map(
        on_device,
        mesh=mesh,
        in_specs=(
            P(("gz", "row", "col"), None, None),
            P(("gz", "row", "col"), None, None),
            P(("gz", "row", "col"), None, None),
            P(("gz", "row", "col"), None),
            P("gz", "col", None),
            P("gz", "row", "col"),
            P("gz", "col", "row"),
            P("col", None),
            P("row", "col"),
        ),
        out_specs=(P(("gz", "row", "col"), None, None), P("gz", "col", None), P("col", None)),
        check_vma=False,
    )
```

time: 515 us -> 90.7 us (0.18)
  waiting for transfers between devices: 420 us -> 0 us
  Pallas kernels: 0 us -> 89.9 us
  blocking collectives: 46.2 us -> 0 us
  matrix products: 21.6 us -> 0 us
  between operations: 13.9 us -> 0.64 us
  local copies, waits for them, and re-layouts: 6.92 us -> 0 us
    psum x5 -> x0, waiting for transfers between devices: 420 us -> none  [the longest x1 179 us: on_device(): root_update = lax.psum(root_terms, ('gz', 'row'))]
    pallas_call x0 -> x2, Pallas kernels: none -> 89.9 us  [the longest x1 85.8 us: on_device(): pl.pallas_call(kernel, out_shape=(jax.ShapeDtypeStruct((NL * N, NRHS), BF...]
    psum x2 -> x0, blocking collectives: 33.4 us -> none  [the longest x1 16.9 us: on_device(): root_half = lax.psum(root_terms_fwd, 'col').astype(jnp.bfloat16)]
    dot_general x9 -> x0, matrix products: 21.6 us -> none  [the longest x1 6.76 us: on_device(): jnp.einsum('lji,ljk->lik', inv_leaf, leaf_back, preferred_element_type=jn...]
    all_gather x1 -> x0, blocking collectives: 12.8 us -> none  [on_device(): lax.all_gather(solve_grid.astype(jnp.bfloat16), 'col', axis=0, tiled=True)]
    unnamed x17 -> x0, local copies, waits for them, and re-layouts: 6.75 us -> none
  transfers between devices with their start and end apart: 5 -> 0, of which waited for: 5 -> 0; matrix products, arithmetic and copies ran while one was open for 0% -> 0% of each run, Pallas kernels for 0% -> 0%
where the time goes in v2:
time: 90.7 us; the launch traced here: 90.5 us
  Pallas kernels  89.9 us (99%)
    pallas_call x1, Pallas kernels, on_device(): pl.pallas_call(kernel, out_shape=(jax.ShapeDtypeStruct((NL * N, NRHS), BF...  85.8 us
    pallas_call x1, Pallas kernels, on_device(): pl.pallas_call(leaves_back, out_shape=(jax.ShapeDtypeStruct((NL, N, NRHS)...  4.05 us

profile of v2, /device:TPU:1, one launch (start us, length us, event | category | flops | bytes accessed | tf_op | source)
XLA Modules:
  0.0 90.5 jit_solution(18044675764791945380)
XLA Ops:
  0.6 85.8 %solve.1 = (bf16[2048,256]{1,0:T(8,128)(2,1)}, bf16[384,256]{1,0:T(8,128)(2,1)}, bf16[256,256]{1,0:T(8,128)(2,1)}) custom-call(bf16[8,256,256]{2,1,0:T(8,128)(2,1)} %rhs_leaf.1, bf16[8,256,256]{2,1,0:T(8,128)(2,1)} %inv_leaf.3, bf16[8,1536,256]{2,1,0:T(8,128)(2,1)} %couple_leaf.1, s32[8,12]{1,0:T(8,128)} %pattern.1, bf16[1,384,256]{2,1,0:T(8,128)(2,1)} %rhs_grid.1, ...), custom_call_target="tpu_custom_call" | custom-call | flops 4200000000 | bytes 13000000 | tf_op jit(solution)/shard_map/solve/pallas_call | solution.py:396
  86.5 4.1 %leaves_back.1 = (f32[8,256,256]{2,1,0:T(8,128)}, f32[1,384,256]{2,1,0:T(8,128)}, f32[256,256]{1,0:T(8,128)}) custom-call(bf16[8,256,256]{2,1,0:T(8,128)(2,1)} %inv_leaf.3, bf16[2048,256]{1,0:T(8,128)(2,1)} %get-tuple-element.6.res_leaf, bf16[384,256]{1,0:T(8,128)(2,1)} %get-tuple-element.7.top, bf16[256,256]{1,0:T(8,128)(2,1)} %get-tuple-element.8.root), custom_call_target="tpu_custom_call" | custom-call | flops 270000000 | bytes 4800000 | tf_op jit(solution)/shard_map/leaves_back/pallas_call | solution.py:431

commit v3 on v2

--- a/solution.py
+++ b/solution.py
@@ -231,17 +231,6 @@
         from_z = rows(lax.rem(gz - k + 16, 16), SLICE)
         zpass.append(remote(blocks.at[:, from_z], blocks.at[:, from_z], sC.at[k + 1], rC.at[k + 1], sibling))
         start(zpass[-1:])
-    arrived(gsend, y <= x)
-
-    @pl.when(y <= x)
-    def _():
-        for a in range(4):
-            bsnd[a] = dot(cg[a], lg[...]).astype(BF16)
-
-    bsend = [
-        remote(bsnd.at[lax.rem(x + k, 4)], rcvb.at[k], sB.at[k], rB.at[k], xpart(k)) for k in range(1, 4)
-    ]
-    start(bsend, y <= x)
     arrived(a4)
     v = ut[mine, :]
     for k in range(1, 16):
@@ -251,6 +240,17 @@
     rcv5[here] = w
     a5 = [remote(wsnd, rcv5.at[here], s5.at[k], r5.at[k], ppart(k)) for k in range(1, 16)]
     start(a5)
+    arrived(gsend, y <= x)
+
+    @pl.when(y <= x)
+    def _():
+        for a in range(4):
+            bsnd[a] = dot(cg[a], lg[...]).astype(BF16)
+
+    bsend = [
+        remote(bsnd.at[lax.rem(x + k, 4)], rcvb.at[k], sB.at[k], rB.at[k], xpart(k)) for k in range(1, 4)
+    ]
+    start(bsend, y <= x)
     arrived(a8)
     hpart[my_piece, :] += rcv8[1].astype(F32) + rcv8[2].astype(F32) + rcv8[3].astype(F32)
     arrived(zpass)
@@ -314,7 +314,7 @@
     home = rows(y * 4 + x, GP)
     xg[home, :] = h.astype(BF16)
     a9 = [remote(xg.at[home], xg.at[home], s9.at[k], r9.at[k], ppart(k)) for k in range(1, 16)]
-    start(a9)
+    start([a9[k - 1] for k in (4, 8, 12, 1, 3, 5, 7, 9, 11, 13, 15, 2, 6, 10, 14)])
     stores = [pltpu.make_async_copy(rt.at[:, rows(y, RB)], out_root, out_sems.at[2])]
     stores[0].start()
     odd = lax.rem(y, 2) == 1

time: 90.7 us -> 86.1 us (0.949)
  Pallas kernels: 89.9 us -> 85.3 us
    pallas_call x1, Pallas kernels: 85.8 us -> 81.2 us  [on_device(): pl.pallas_call(kernel, out_shape=(jax.ShapeDtypeStruct((NL * N, NRHS), BF...]
where the time goes in v3:
time: 86.1 us; the launch traced here: 85.9 us
  Pallas kernels  85.3 us (99%)
    pallas_call x1, Pallas kernels, on_device(): pl.pallas_call(kernel, out_shape=(jax.ShapeDtypeStruct((NL * N, NRHS), BF...  81.2 us
    pallas_call x1, Pallas kernels, on_device(): pl.pallas_call(leaves_back, out_shape=(jax.ShapeDtypeStruct((NL, N, NRHS)...  4.05 us

profile of v3, /device:TPU:1, one launch (start us, length us, event | category | flops | bytes accessed | tf_op | source)
XLA Modules:
  0.0 85.9 jit_solution(15829529732832259419)
XLA Ops:
  0.6 81.2 %solve.1 = (bf16[2048,256]{1,0:T(8,128)(2,1)}, bf16[384,256]{1,0:T(8,128)(2,1)}, bf16[256,256]{1,0:T(8,128)(2,1)}) custom-call(bf16[8,256,256]{2,1,0:T(8,128)(2,1)} %rhs_leaf.1, bf16[8,256,256]{2,1,0:T(8,128)(2,1)} %inv_leaf.3, bf16[8,1536,256]{2,1,0:T(8,128)(2,1)} %couple_leaf.1, s32[8,12]{1,0:T(8,128)} %pattern.1, bf16[1,384,256]{2,1,0:T(8,128)(2,1)} %rhs_grid.1, ...), custom_call_target="tpu_custom_call" | custom-call | flops 4200000000 | bytes 13000000 | tf_op jit(solution)/shard_map/solve/pallas_call | solution.py:396
  81.9 4.1 %leaves_back.1 = (f32[8,256,256]{2,1,0:T(8,128)}, f32[1,384,256]{2,1,0:T(8,128)}, f32[256,256]{1,0:T(8,128)}) custom-call(bf16[8,256,256]{2,1,0:T(8,128)(2,1)} %inv_leaf.3, bf16[2048,256]{1,0:T(8,128)(2,1)} %get-tuple-element.6.res_leaf, bf16[384,256]{1,0:T(8,128)(2,1)} %get-tuple-element.7.top, bf16[256,256]{1,0:T(8,128)(2,1)} %get-tuple-element.8.root), custom_call_target="tpu_custom_call" | custom-call | flops 270000000 | bytes 4800000 | tf_op jit(solution)/shard_map/leaves_back/pallas_call | solution.py:431

commit v4 on v3

--- a/solution.py
+++ b/solution.py
@@ -340,6 +340,8 @@
             arrived(a9[k - 1:k], jnp.logical_not(odd))
         elif dy == 3:
             arrived(a9[k - 1:k], odd)
+    stores.append(pltpu.make_async_copy(xg.at[rows(y, GB)], out_top, out_sems.at[3]))
+    stores[-1].start()
     rest = pl.ds(pl.multiple_of((1 - y // 2) * HALF, HALF), HALF)
     for g in range(2):
         gs = slice(g * 4 * N, (g + 1) * 4 * N)
@@ -347,8 +349,6 @@
         back[gs, :] = (ol[gs, :] - t).astype(BF16)
         stores.append(pltpu.make_async_copy(back.at[gs], out_back.at[gs], out_sems.at[g]))
         stores[-1].start()
-    stores.append(pltpu.make_async_copy(xg.at[rows(y, GB)], out_top, out_sems.at[3]))
-    stores[-1].start()
     finish()
     for c in stores:
         c.wait()
@@ -376,14 +376,15 @@
         sol[l] = dot_tn(il[l], bk[l])
         copies.append(pltpu.make_async_copy(sol.at[l], out_leaf.at[l], sems.at[l]))
         copies[-1].start()
-    for c in small:
-        c.wait()
-    og[...] = tp[...].astype(F32)
-    copies.append(pltpu.make_async_copy(og, out_grid.at[0], sems.at[NL]))
-    copies[-1].start()
-    oroot[...] = rt[...].astype(F32).T
-    copies.append(pltpu.make_async_copy(oroot, out_root, sems.at[NL + 1]))
-    copies[-1].start()
+        if l == 3:
+            for c in small:
+                c.wait()
+            og[...] = tp[...].astype(F32)
+            copies.append(pltpu.make_async_copy(og, out_grid.at[0], sems.at[NL]))
+            copies[-1].start()
+            oroot[...] = rt[...].astype(F32).T
+            copies.append(pltpu.make_async_copy(oroot, out_root, sems.at[NL + 1]))
+            copies[-1].start()
     for c in copies:
         c.wait()
 

time: 86.1 us -> 85.9 us (level)
  no operation moved by 1% of the time
where the time goes in v4:
time: 85.9 us; the launch traced here: 85.8 us
  Pallas kernels  85.1 us (99%)
    pallas_call x1, Pallas kernels, on_device(): pl.pallas_call(kernel, out_shape=(jax.ShapeDtypeStruct((NL * N, NRHS), BF...  81.2 us
    pallas_call x1, Pallas kernels, on_device(): pl.pallas_call(leaves_back, out_shape=(jax.ShapeDtypeStruct((NL, N, NRHS)...  3.94 us

profile of v4, /device:TPU:1, one launch (start us, length us, event | category | flops | bytes accessed | tf_op | source)
XLA Modules:
  0.0 85.8 jit_solution(10986107766926848912)
XLA Ops:
  0.6 81.2 %solve.1 = (bf16[2048,256]{1,0:T(8,128)(2,1)}, bf16[384,256]{1,0:T(8,128)(2,1)}, bf16[256,256]{1,0:T(8,128)(2,1)}) custom-call(bf16[8,256,256]{2,1,0:T(8,128)(2,1)} %rhs_leaf.1, bf16[8,256,256]{2,1,0:T(8,128)(2,1)} %inv_leaf.3, bf16[8,1536,256]{2,1,0:T(8,128)(2,1)} %couple_leaf.1, s32[8,12]{1,0:T(8,128)} %pattern.1, bf16[1,384,256]{2,1,0:T(8,128)(2,1)} %rhs_grid.1, ...), custom_call_target="tpu_custom_call" | custom-call | flops 4200000000 | bytes 13000000 | tf_op jit(solution)/shard_map/solve/pallas_call | solution.py:397
  81.8 3.9 %leaves_back.1 = (f32[8,256,256]{2,1,0:T(8,128)}, f32[1,384,256]{2,1,0:T(8,128)}, f32[256,256]{1,0:T(8,128)}) custom-call(bf16[8,256,256]{2,1,0:T(8,128)(2,1)} %inv_leaf.3, bf16[2048,256]{1,0:T(8,128)(2,1)} %get-tuple-element.6.res_leaf, bf16[384,256]{1,0:T(8,128)(2,1)} %get-tuple-element.7.top, bf16[256,256]{1,0:T(8,128)(2,1)} %get-tuple-element.8.root), custom_call_target="tpu_custom_call" | custom-call | flops 270000000 | bytes 4800000 | tf_op jit(solution)/shard_map/leaves_back/pallas_call | solution.py:432

commit v5 on v3

--- a/solution.py
+++ b/solution.py
@@ -141,9 +141,9 @@
         if jj == 0:
             own1[...] = acc
         snd1[rows(jj, GB), :] = acc.astype(BF16)
-        if jj == 1:
+        if jj == 0:
             pl.semaphore_wait(barrier, 30)
-        for sent in {0: (), 1: (0, 1), 2: (2,), 3: (3,)}[jj]:
+        for sent in (jj,):
             for dx in range(4):
                 k = dx * 4 + sent
                 if k == 0:

time: 86.1 us -> 87.7 us (1.019)
  Pallas kernels: 85.3 us -> 86.9 us
    pallas_call x1, Pallas kernels: 81.2 us -> 82.8 us  [on_device(): pl.pallas_call(kernel, out_shape=(jax.ShapeDtypeStruct((NL * N, NRHS), BF...]
where the time goes in v5:
time: 87.7 us; the launch traced here: 87.5 us
  Pallas kernels  86.9 us (99%)
    pallas_call x1, Pallas kernels, on_device(): pl.pallas_call(kernel, out_shape=(jax.ShapeDtypeStruct((NL * N, NRHS), BF...  82.8 us
    pallas_call x1, Pallas kernels, on_device(): pl.pallas_call(leaves_back, out_shape=(jax.ShapeDtypeStruct((NL, N, NRHS)...  4.05 us

profile of v5, /device:TPU:1, one launch (start us, length us, event | category | flops | bytes accessed | tf_op | source)
XLA Modules:
  0.0 87.5 jit_solution(4460501083666631777)
XLA Ops:
  0.6 82.8 %solve.1 = (bf16[2048,256]{1,0:T(8,128)(2,1)}, bf16[384,256]{1,0:T(8,128)(2,1)}, bf16[256,256]{1,0:T(8,128)(2,1)}) custom-call(bf16[8,256,256]{2,1,0:T(8,128)(2,1)} %rhs_leaf.1, bf16[8,256,256]{2,1,0:T(8,128)(2,1)} %inv_leaf.3, bf16[8,1536,256]{2,1,0:T(8,128)(2,1)} %couple_leaf.1, s32[8,12]{1,0:T(8,128)} %pattern.1, bf16[1,384,256]{2,1,0:T(8,128)(2,1)} %rhs_grid.1, ...), custom_call_target="tpu_custom_call" | custom-call | flops 4200000000 | bytes 13000000 | tf_op jit(solution)/shard_map/solve/pallas_call | solution.py:396
  83.5 4.1 %leaves_back.1 = (f32[8,256,256]{2,1,0:T(8,128)}, f32[1,384,256]{2,1,0:T(8,128)}, f32[256,256]{1,0:T(8,128)}) custom-call(bf16[8,256,256]{2,1,0:T(8,128)(2,1)} %inv_leaf.3, bf16[2048,256]{1,0:T(8,128)(2,1)} %get-tuple-element.6.res_leaf, bf16[384,256]{1,0:T(8,128)(2,1)} %get-tuple-element.7.top, bf16[256,256]{1,0:T(8,128)(2,1)} %get-tuple-element.8.root), custom_call_target="tpu_custom_call" | custom-call | flops 270000000 | bytes 4800000 | tf_op jit(solution)/shard_map/leaves_back/pallas_call | solution.py:431
